TPU v7x, 256 devices: a whole 4x4x8 slice. The times are simulated.
256 devices in a mesh: gx: 16 (over z, core), gy: 16 (over y, x).
Axes of the slice: x: 4, y: 4, z: 8, core: 2. Of those that a mesh axis runs over, the one named last changes fastest.
Arguments:
- right_side: float32 [128, 128, 8, 512], P('gx', 'gy'), may hold values from -9 to 9
- kappa_sq: float32 [128, 128, 512], P('gx', 'gy'), may hold values from 0.01 to 2
- coarse_inverse: float32 [4096, 256], P('gx'), may hold values from -0.25 to 32, as said below
Outputs:
- iterate: float32 [128, 128, 8, 512], P('gx', 'gy')
- residual: float32 [128, 128, 8, 512], P('gx', 'gy')
Inputs may be any that keep to these rules, and one draw needn't show every extreme that they name: `coarse_inverse`: each slab's block of 256 rows is a symmetric 256 x 256 matrix; its off-diagonal entries lie within -0.25 to 0.25 and its diagonal entries within 8 to 32.
All inputs are finite; a program needn't handle non-finite values.
Results may differ from a plain program's by a relative error of at most 0.0003.
Values sent between devices are 32-bit elements; how exact they have to be, the bound alone decides.
No kernel may reach another device: no remote copies, remote signals or barrier semaphores. Data moves between devices by JAX's collectives and lax.ppermute only.
A program may use at most 64 MiB of HBM per device.

v0:
```python
import jax
import jax.numpy as jnp
from jax import lax
from jax.sharding import PartitionSpec as P

NCD = 16
ITERS = 2
relax_weight = 2.0 / 3.0


def with_halo(block, sides, width):
    for axis, dim in sides:
        count = lax.axis_size(axis)
        forward = [(i, i + 1) for i in range(count - 1)]
        backward = [(target, source) for source, target in forward]
        low = lax.ppermute(
            lax.slice_in_dim(block, block.shape[dim] - width, None, axis=dim), axis, forward
        )
        high = lax.ppermute(lax.slice_in_dim(block, 0, width, axis=dim), axis, backward)
        block = jnp.concatenate([low, block, high], axis=dim)
    return block


def stencil(padded, field, diag_shift):
    padded = jnp.pad(padded, ((0, 0), (0, 0), (0, 0), (1, 1)))
    beside = padded[2:, 1:-1, :, 1:-1] + padded[:-2, 1:-1, :, 1:-1]
    beside = beside + padded[1:-1, 2:, :, 1:-1] + padded[1:-1, :-2, :, 1:-1]
    beside = beside + padded[1:-1, 1:-1, :, 2:] + padded[1:-1, 1:-1, :, :-2]
    return diag_shift * field - beside


def apply_operator(field, diag_shift):
    padded = with_halo(field, (("gx", 0), ("gy", 1)), 1)
    return stencil(padded, field, diag_shift)


def jacobi_sweep(correction, source, diag_shift):
    return (
        correction + relax_weight * (source - apply_operator(correction, diag_shift)) / diag_shift
    )


def coarse_solve(defect, coarse_inverse):
    width_x, width_y, probes, depth = defect.shape
    zblock = depth // NCD
    blocks = defect.reshape(width_x, width_y, probes, NCD, zblock)
    local_means = jnp.mean(blocks, axis=(0, 1, 4))
    row_start = lax.axis_index("gy") * NCD
    own_rows = lax.dynamic_slice_in_dim(coarse_inverse, row_start, NCD, 0)
    return lax.dot_general(
        lax.all_gather(local_means, "gy", axis=1, tiled=True),
        own_rows,
        (((1,), (1,)), ((), ())),
        precision=lax.Precision.HIGHEST,
        preferred_element_type=jnp.float32,
    )


def prolong(coarse_values, shape):
    width_x, width_y, probes, depth = shape
    zblock = depth // NCD
    spread = jnp.broadcast_to(
        coarse_values[None, None, :, :, None], (width_x, width_y, probes, NCD, zblock)
    )
    return spread.reshape(shape)


def precondition(source, diag_shift, coarse_inverse):
    correction = relax_weight * source / diag_shift
    correction = jacobi_sweep(correction, source, diag_shift)
    defect = source - apply_operator(correction, diag_shift)
    coarse_values = coarse_solve(defect, coarse_inverse)
    coarse_field = prolong(coarse_values, source.shape)
    correction = correction + coarse_field
    correction = jacobi_sweep(correction, source, diag_shift)
    return jacobi_sweep(correction, source, diag_shift)


def probe_dot(first, second):
    return jnp.sum(first * second, axis=(0, 1, 3))


def per_probe(values):
    return values[None, None, :, None]


def energy_sum(residual, precond):
    return lax.psum(probe_dot(residual, precond), ("gx", "gy"))


def body(right_side, kappa_sq, coarse_inverse):
    diag_shift = (6.0 + kappa_sq)[:, :, None, :]
    iterate = jnp.zeros_like(right_side)
    residual = right_side
    precond = precondition(residual, diag_shift, coarse_inverse)
    search = precond
    energy = energy_sum(residual, precond)
    for iteration in range(ITERS):
        op_image = apply_operator(search, diag_shift)
        curvature = lax.psum(probe_dot(search, op_image), ("gx", "gy"))
        step_size = energy / curvature
        iterate = iterate + per_probe(step_size) * search
        residual = residual - per_probe(step_size) * op_image
        if iteration + 1 < ITERS:
            precond = precondition(residual, diag_shift, coarse_inverse)
            energy_next = energy_sum(residual, precond)
            search = precond + per_probe(energy_next / energy) * search
            energy = energy_next
    return (iterate, residual)


def solution(mesh):
    placed = (P("gx", "gy", None, None), P("gx", "gy", None), P("gx", None))
    return jax.shard_map(
        body,
        mesh=mesh,
        in_specs=placed,
        out_specs=(P("gx", "gy", None, None), P("gx", "gy", None, None)),
        check_vma=False,
    )
```

profile of v0, /device:TPU:1, one launch (start us, length us, event | category | flops | bytes accessed | tf_op | source)
XLA Modules:
  0.0 519.5 jit_solution(6656495104835346042)
XLA Ops:
  1.6 1.4 multiply_divide_fusion.1
  3.1 4.9 collective-permute-start.1
  8.0 1.9 collective-permute-start
  10.0 4.3 collective-permute-done
  14.3 3.3 collective-permute-start.3
  19.8 3.8 collective-permute-done.2
  25.0 4.1 collective-permute-start.5
  29.1 1.9 collective-permute-start.4
  31.0 4.3 collective-permute-done.4
  35.4 3.1 collective-permute-start.7
  40.8 3.8 collective-permute-done.6
  46.0 21.1 %all-gather = f32[16,16,8]{1,2,0:T(8,128)S(1)} all-gather(f32[1,16,8]{1,2,0:T(8,128)S(1)} %multiply_bitcast_fusion.1), channel_id=1, replica_groups=mesh['gx'=16,'gy'=16] {'gy'}, dimensions={0}, use_global_device_ids=true | all-gather | bytes 8704 | tf_op jit(solution)/shard_map/all_gather | solution.py:51
  67.7 9.0 %collective-permute-start.9 = (f32[1,8,8,512]{3,2,1,0:T(8,128)S(1)}, f32[1,8,8,512]{3,2,1,0:T(8,128)S(1)}, u32[]{:S(2)}, u32[]{:S(2)}) collective-permute-start(f32[1,8,8,512]{3,2,1,0:T(8,128)S(1)} %get-tuple-element.47), channel_id=1, source_target_pairs={{0,16},{16,32},{32,48},{48,64},{64,80},{80,96},{96,112},{112,128},... | collective-permute-start | bytes 393224 | tf_op jit(solution)/shard_map/ppermute | solution.py:16
  76.6 1.9 collective-permute-start.8
  78.6 4.3 collective-permute-done.8
  82.9 1.8 collective-permute-start.11
  87.0 3.8 collective-permute-done.10
  92.2 4.7 collective-permute-start.13
  96.8 1.9 collective-permute-start.12
  98.8 4.3 collective-permute-done.12
  103.1 2.8 collective-permute-start.15
  106.0 1.3 collective-permute-start.14
  108.2 3.8 collective-permute-done.14
  113.4 4.0 collective-permute-start.17
  117.4 1.9 collective-permute-start.16
  119.3 4.3 collective-permute-done.16
  123.7 4.9 collective-permute-start.19
  130.8 3.8 collective-permute-done.18
  135.2 1.8 multiply_reduce_fusion.2
  137.0 84.1 %all-reduce.10 = (f32[8]{0:T(128)S(1)}, f32[8]{0:T(128)S(1)}) all-reduce(f32[8]{0:T(128)S(1)} %get-tuple-element.3, f32[8]{0:T(128)S(1)} %get-tuple-element.2), channel_id=1, replica_groups=mesh['gx'=16,'gy'=16] {'gx','gy'}, use_global_device_ids=true, to_apply=%region_3.4 | all-reduce | flops 16 | bytes 128 | tf_op jit(solution)/shard_map/psum | solution.py:88
  221.7 1.6 multiply_divide_fusion
  223.3 1.9 collective-permute-start.21
  225.2 2.4 collective-permute-start.20
  227.6 3.9 collective-permute-done.20
  231.5 2.4 collective-permute-start.23
  234.0 1.3 collective-permute-start.22
  236.2 3.8 collective-permute-done.22
  241.3 4.9 collective-permute-start.25
  246.2 1.9 collective-permute-start.24
  248.2 4.3 collective-permute-done.24
  252.5 2.2 collective-permute-start.27
  257.0 4.3 collective-permute-done.26
  264.1 21.4 %all-gather.1 = f32[16,16,8]{1,2,0:T(8,128)S(1)} all-gather(f32[1,16,8]{1,2,0:T(8,128)S(1)} %multiply_bitcast_fusion), channel_id=1, replica_groups=mesh['gx'=16,'gy'=16] {'gy'}, dimensions={0}, use_global_device_ids=true | all-gather | bytes 8704 | tf_op jit(solution)/shard_map/all_gather | solution.py:51
  289.0 9.9 %collective-permute-start.29 = (f32[1,8,8,512]{3,2,1,0:T(8,128)S(1)}, f32[1,8,8,512]{3,2,1,0:T(8,128)S(1)}, u32[]{:S(2)}, u32[]{:S(2)}) collective-permute-start(f32[1,8,8,512]{3,2,1,0:T(8,128)S(1)} %get-tuple-element.37), channel_id=1, source_target_pairs={{0,16},{16,32},{32,48},{48,64},{64,80},{80,96},{96,112},{112,128},... | collective-permute-start | bytes 393224 | tf_op jit(solution)/shard_map/ppermute | solution.py:16
  298.9 1.9 collective-permute-start.28
  300.9 4.3 collective-permute-done.28
  305.2 1.3 collective-permute-start.31
  308.8 3.8 collective-permute-done.30
  314.0 4.5 collective-permute-start.33
  318.5 1.9 collective-permute-start.32
  320.4 4.3 collective-permute-done.32
  324.8 3.8 collective-permute-start.35
  330.8 3.8 collective-permute-done.34
  335.2 1.8 multiply_reduce_fusion.1
  337.0 79.8 %psum.30 = f32[8]{0:T(128)S(1)} all-reduce(f32[8]{0:T(128)S(1)} %get-tuple-element.8), channel_id=1, replica_groups=mesh['gx'=16,'gy'=16] {'gx','gy'}, use_global_device_ids=true, to_apply=%region_9.10 | all-reduce | flops 8 | bytes 64 | tf_op jit(solution)/shard_map/psum | solution.py:88
  416.8 1.5 multiply_add_fusion.1
  418.3 2.0 collective-permute-start.37
  420.3 2.3 collective-permute-start.36
  422.7 3.9 collective-permute-done.36
  426.7 1.6 collective-permute-start.39
  430.5 3.8 collective-permute-done.38
  434.9 1.7 multiply_reduce_fusion
  436.6 79.8 %psum.31 = f32[8]{0:T(128)S(1)} all-reduce(f32[8]{0:T(128)S(1)} %get-tuple-element.6), channel_id=1, replica_groups=mesh['gx'=16,'gy'=16] {'gx','gy'}, use_global_device_ids=true, to_apply=%region_11.12 | all-reduce | flops 8 | bytes 64 | tf_op jit(solution)/shard_map/psum | solution.py:100
  516.4 3.1 multiply_subtract_fusion
  (99 shorter events, 38.1 us)
Async XLA Ops:
  0.6 66.5 %copy-start = (f32[256,256]{1,0:T(8,128)S(1)}, f32[256,256]{1,0:T(8,128)}, u32[]{:S(2)}) copy-start(f32[256,256]{1,0:T(8,128)} %param.5) | copy-start | bytes 786436
  3.1 6.9 %collective-permute-start.1 = (f32[1,8,8,512]{3,2,1,0:T(8,128)S(1)}, f32[1,8,8,512]{3,2,1,0:T(8,128)S(1)}, u32[]{:S(2)}, u32[]{:S(2)}) collective-permute-start(f32[1,8,8,512]{3,2,1,0:T(8,128)S(1)} %get-tuple-element.51), channel_id=1, source_target_pairs={{0,16},{16,32},{32,48},{48,64},{64,80},{80,96},{96,112},{112,128},... | collective-permute-start | bytes 393224 | tf_op jit(solution)/shard_map/ppermute | solution.py:16
  8.0 6.3 %collective-permute-start = (f32[1,8,8,512]{3,2,1,0:T(8,128)S(1)}, f32[1,8,8,512]{3,2,1,0:T(8,128)S(1)}, u32[]{:S(2)}, u32[]{:S(2)}) collective-permute-start(f32[1,8,8,512]{3,2,1,0:T(8,128)S(1)} %get-tuple-element.52), channel_id=1, source_target_pairs={{16,0},{32,16},{48,32},{64,48},{80,64},{96,80},{112,96},{128,112},... | collective-permute-start | bytes 393224 | tf_op jit(solution)/shard_map/ppermute | solution.py:19
  14.3 9.9 %copy-start.1 = (f32[8,8,8,512]{3,2,1,0:T(8,128)S(1)}, f32[8,8,8,512]{3,2,1,0:T(8,128)}, u32[]{:S(2)}) copy-start(f32[8,8,8,512]{3,2,1,0:T(8,128)} %param.3) | copy-start | bytes 3145732
  14.3 5.5 %collective-permute-start.3 = (f32[10,1,8,512]{3,2,1,0:T(8,128)S(1)}, f32[10,1,8,512]{3,2,1,0:T(8,128)S(1)}, u32[]{:S(2)}, u32[]{:S(2)}) collective-permute-start(f32[10,1,8,512]{3,2,1,0:T(8,128)S(1)} %get-tuple-element.31), channel_id=1, source_target_pairs={{0,1},{1,2},{2,3},{3,4},{4,5},{5,6},{6,7},{7,8},{8,9},{9,10},{10,1... | collective-permute-start | bytes 491528 | tf_op jit(solution)/shard_map/ppermute | solution.py:16
  17.6 6.1 %collective-permute-start.2 = (f32[10,1,8,512]{3,2,1,0:T(8,128)S(1)}, f32[10,1,8,512]{3,2,1,0:T(8,128)S(1)}, u32[]{:S(2)}, u32[]{:S(2)}) collective-permute-start(f32[10,1,8,512]{3,2,1,0:T(8,128)S(1)} %get-tuple-element.32), channel_id=1, source_target_pairs={{1,0},{2,1},{3,2},{4,3},{5,4},{6,5},{7,6},{8,7},{9,8},{10,9},{11,1... | collective-permute-start | bytes 491528 | tf_op jit(solution)/shard_map/ppermute | solution.py:19
  25.0 6.0 %collective-permute-start.5 = (f32[1,8,8,512]{3,2,1,0:T(8,128)S(1)}, f32[1,8,8,512]{3,2,1,0:T(8,128)S(1)}, u32[]{:S(2)}, u32[]{:S(2)}) collective-permute-start(f32[1,8,8,512]{3,2,1,0:T(8,128)S(1)} %get-tuple-element.49), channel_id=1, source_target_pairs={{0,16},{16,32},{32,48},{48,64},{64,80},{80,96},{96,112},{112,128},... | collective-permute-start | bytes 393224 | tf_op jit(solution)/shard_map/ppermute | solution.py:16
  29.1 6.3 %collective-permute-start.4 = (f32[1,8,8,512]{3,2,1,0:T(8,128)S(1)}, f32[1,8,8,512]{3,2,1,0:T(8,128)S(1)}, u32[]{:S(2)}, u32[]{:S(2)}) collective-permute-start(f32[1,8,8,512]{3,2,1,0:T(8,128)S(1)} %get-tuple-element.50), channel_id=1, source_target_pairs={{16,0},{32,16},{48,32},{64,48},{80,64},{96,80},{112,96},{128,112},... | collective-permute-start | bytes 393224 | tf_op jit(solution)/shard_map/ppermute | solution.py:19
  35.4 5.4 %collective-permute-start.7 = (f32[10,1,8,512]{3,2,1,0:T(8,128)S(1)}, f32[10,1,8,512]{3,2,1,0:T(8,128)S(1)}, u32[]{:S(2)}, u32[]{:S(2)}) collective-permute-start(f32[10,1,8,512]{3,2,1,0:T(8,128)S(1)} %get-tuple-element.29), channel_id=1, source_target_pairs={{0,1},{1,2},{2,3},{3,4},{4,5},{5,6},{6,7},{7,8},{8,9},{9,10},{10,1... | collective-permute-start | bytes 491528 | tf_op jit(solution)/shard_map/ppermute | solution.py:16
  38.5 6.1 %collective-permute-start.6 = (f32[10,1,8,512]{3,2,1,0:T(8,128)S(1)}, f32[10,1,8,512]{3,2,1,0:T(8,128)S(1)}, u32[]{:S(2)}, u32[]{:S(2)}) collective-permute-start(f32[10,1,8,512]{3,2,1,0:T(8,128)S(1)} %get-tuple-element.30), channel_id=1, source_target_pairs={{1,0},{2,1},{3,2},{4,3},{5,4},{6,5},{7,6},{8,7},{9,8},{10,9},{11,1... | collective-permute-start | bytes 491528 | tf_op jit(solution)/shard_map/ppermute | solution.py:19
  67.7 10.9 %collective-permute-start.9 = (f32[1,8,8,512]{3,2,1,0:T(8,128)S(1)}, f32[1,8,8,512]{3,2,1,0:T(8,128)S(1)}, u32[]{:S(2)}, u32[]{:S(2)}) collective-permute-start(f32[1,8,8,512]{3,2,1,0:T(8,128)S(1)} %get-tuple-element.47), channel_id=1, source_target_pairs={{0,16},{16,32},{32,48},{48,64},{64,80},{80,96},{96,112},{112,128},... | collective-permute-start | bytes 393224 | tf_op jit(solution)/shard_map/ppermute | solution.py:16
  76.6 6.3 %collective-permute-start.8 = (f32[1,8,8,512]{3,2,1,0:T(8,128)S(1)}, f32[1,8,8,512]{3,2,1,0:T(8,128)S(1)}, u32[]{:S(2)}, u32[]{:S(2)}) collective-permute-start(f32[1,8,8,512]{3,2,1,0:T(8,128)S(1)} %get-tuple-element.48), channel_id=1, source_target_pairs={{16,0},{32,16},{48,32},{64,48},{80,64},{96,80},{112,96},{128,112},... | collective-permute-start | bytes 393224 | tf_op jit(solution)/shard_map/ppermute | solution.py:19
  82.9 4.1 collective-permute-start.11
  84.8 6.1 %collective-permute-start.10 = (f32[10,1,8,512]{3,2,1,0:T(8,128)S(1)}, f32[10,1,8,512]{3,2,1,0:T(8,128)S(1)}, u32[]{:S(2)}, u32[]{:S(2)}) collective-permute-start(f32[10,1,8,512]{3,2,1,0:T(8,128)S(1)} %get-tuple-element.28), channel_id=1, source_target_pairs={{1,0},{2,1},{3,2},{4,3},{5,4},{6,5},{7,6},{8,7},{9,8},{10,9},{11,1... | collective-permute-start | bytes 491528 | tf_op jit(solution)/shard_map/ppermute | solution.py:19
  92.2 6.6 %collective-permute-start.13 = (f32[1,8,8,512]{3,2,1,0:T(8,128)S(1)}, f32[1,8,8,512]{3,2,1,0:T(8,128)S(1)}, u32[]{:S(2)}, u32[]{:S(2)}) collective-permute-start(f32[1,8,8,512]{3,2,1,0:T(8,128)S(1)} %get-tuple-element.45), channel_id=1, source_target_pairs={{0,16},{16,32},{32,48},{48,64},{64,80},{80,96},{96,112},{112,128},... | collective-permute-start | bytes 393224 | tf_op jit(solution)/shard_map/ppermute | solution.py:16
  96.8 6.3 %collective-permute-start.12 = (f32[1,8,8,512]{3,2,1,0:T(8,128)S(1)}, f32[1,8,8,512]{3,2,1,0:T(8,128)S(1)}, u32[]{:S(2)}, u32[]{:S(2)}) collective-permute-start(f32[1,8,8,512]{3,2,1,0:T(8,128)S(1)} %get-tuple-element.46), channel_id=1, source_target_pairs={{16,0},{32,16},{48,32},{64,48},{80,64},{96,80},{112,96},{128,112},... | collective-permute-start | bytes 393224 | tf_op jit(solution)/shard_map/ppermute | solution.py:19
  103.1 5.1 collective-permute-start.15
  106.0 6.1 %collective-permute-start.14 = (f32[10,1,8,512]{3,2,1,0:T(8,128)S(1)}, f32[10,1,8,512]{3,2,1,0:T(8,128)S(1)}, u32[]{:S(2)}, u32[]{:S(2)}) collective-permute-start(f32[10,1,8,512]{3,2,1,0:T(8,128)S(1)} %get-tuple-element.26), channel_id=1, source_target_pairs={{1,0},{2,1},{3,2},{4,3},{5,4},{6,5},{7,6},{8,7},{9,8},{10,9},{11,1... | collective-permute-start | bytes 491528 | tf_op jit(solution)/shard_map/ppermute | solution.py:19
  113.4 5.9 %collective-permute-start.17 = (f32[1,8,8,512]{3,2,1,0:T(8,128)S(1)}, f32[1,8,8,512]{3,2,1,0:T(8,128)S(1)}, u32[]{:S(2)}, u32[]{:S(2)}) collective-permute-start(f32[1,8,8,512]{3,2,1,0:T(8,128)S(1)} %get-tuple-element.43), channel_id=1, source_target_pairs={{0,16},{16,32},{32,48},{48,64},{64,80},{80,96},{96,112},{112,128},... | collective-permute-start | bytes 393224 | tf_op jit(solution)/shard_map/ppermute | solution.py:16
  117.4 6.3 %collective-permute-start.16 = (f32[1,8,8,512]{3,2,1,0:T(8,128)S(1)}, f32[1,8,8,512]{3,2,1,0:T(8,128)S(1)}, u32[]{:S(2)}, u32[]{:S(2)}) collective-permute-start(f32[1,8,8,512]{3,2,1,0:T(8,128)S(1)} %get-tuple-element.44), channel_id=1, source_target_pairs={{16,0},{32,16},{48,32},{64,48},{80,64},{96,80},{112,96},{128,112},... | collective-permute-start | bytes 393224 | tf_op jit(solution)/shard_map/ppermute | solution.py:19
  123.7 7.1 %collective-permute-start.19 = (f32[10,1,8,512]{3,2,1,0:T(8,128)S(1)}, f32[10,1,8,512]{3,2,1,0:T(8,128)S(1)}, u32[]{:S(2)}, u32[]{:S(2)}) collective-permute-start(f32[10,1,8,512]{3,2,1,0:T(8,128)S(1)} %get-tuple-element.23), channel_id=1, source_target_pairs={{0,1},{1,2},{2,3},{3,4},{4,5},{5,6},{6,7},{7,8},{8,9},{9,10},{10,1... | collective-permute-start | bytes 491528 | tf_op jit(solution)/shard_map/ppermute | solution.py:16
  128.6 6.1 %collective-permute-start.18 = (f32[10,1,8,512]{3,2,1,0:T(8,128)S(1)}, f32[10,1,8,512]{3,2,1,0:T(8,128)S(1)}, u32[]{:S(2)}, u32[]{:S(2)}) collective-permute-start(f32[10,1,8,512]{3,2,1,0:T(8,128)S(1)} %get-tuple-element.24), channel_id=1, source_target_pairs={{1,0},{2,1},{3,2},{4,3},{5,4},{6,5},{7,6},{8,7},{9,8},{10,9},{11,1... | collective-permute-start | bytes 491528 | tf_op jit(solution)/shard_map/ppermute | solution.py:19
  221.1 0.5 copy-start.4
  221.7 1.6 copy-start.2
  223.3 4.3 collective-permute-start.21
  225.2 6.3 %collective-permute-start.20 = (f32[1,8,8,512]{3,2,1,0:T(8,128)S(1)}, f32[1,8,8,512]{3,2,1,0:T(8,128)S(1)}, u32[]{:S(2)}, u32[]{:S(2)}) collective-permute-start(f32[1,8,8,512]{3,2,1,0:T(8,128)S(1)} %get-tuple-element.42), channel_id=1, source_target_pairs={{16,0},{32,16},{48,32},{64,48},{80,64},{96,80},{112,96},{128,112},... | collective-permute-start | bytes 393224 | tf_op jit(solution)/shard_map/ppermute | solution.py:19
  231.5 4.7 collective-permute-start.23
  234.0 6.1 %collective-permute-start.22 = (f32[10,1,8,512]{3,2,1,0:T(8,128)S(1)}, f32[10,1,8,512]{3,2,1,0:T(8,128)S(1)}, u32[]{:S(2)}, u32[]{:S(2)}) collective-permute-start(f32[10,1,8,512]{3,2,1,0:T(8,128)S(1)} %get-tuple-element.22), channel_id=1, source_target_pairs={{1,0},{2,1},{3,2},{4,3},{5,4},{6,5},{7,6},{8,7},{9,8},{10,9},{11,1... | collective-permute-start | bytes 491528 | tf_op jit(solution)/shard_map/ppermute | solution.py:19
  241.3 6.8 %collective-permute-start.25 = (f32[1,8,8,512]{3,2,1,0:T(8,128)S(1)}, f32[1,8,8,512]{3,2,1,0:T(8,128)S(1)}, u32[]{:S(2)}, u32[]{:S(2)}) collective-permute-start(f32[1,8,8,512]{3,2,1,0:T(8,128)S(1)} %get-tuple-element.39), channel_id=1, source_target_pairs={{0,16},{16,32},{32,48},{48,64},{64,80},{80,96},{96,112},{112,128},... | collective-permute-start | bytes 393224 | tf_op jit(solution)/shard_map/ppermute | solution.py:16
  246.2 6.3 %collective-permute-start.24 = (f32[1,8,8,512]{3,2,1,0:T(8,128)S(1)}, f32[1,8,8,512]{3,2,1,0:T(8,128)S(1)}, u32[]{:S(2)}, u32[]{:S(2)}) collective-permute-start(f32[1,8,8,512]{3,2,1,0:T(8,128)S(1)} %get-tuple-element.40), channel_id=1, source_target_pairs={{16,0},{32,16},{48,32},{64,48},{80,64},{96,80},{112,96},{128,112},... | collective-permute-start | bytes 393224 | tf_op jit(solution)/shard_map/ppermute | solution.py:19
  252.5 4.4 collective-permute-start.27
  254.7 6.5 %collective-permute-start.26 = (f32[10,1,8,512]{3,2,1,0:T(8,128)S(1)}, f32[10,1,8,512]{3,2,1,0:T(8,128)S(1)}, u32[]{:S(2)}, u32[]{:S(2)}) collective-permute-start(f32[10,1,8,512]{3,2,1,0:T(8,128)S(1)} %get-tuple-element.20), channel_id=1, source_target_pairs={{1,0},{2,1},{3,2},{4,3},{5,4},{6,5},{7,6},{8,7},{9,8},{10,9},{11,1... | collective-permute-start | bytes 491528 | tf_op jit(solution)/shard_map/ppermute | solution.py:19
  289.0 11.8 %collective-permute-start.29 = (f32[1,8,8,512]{3,2,1,0:T(8,128)S(1)}, f32[1,8,8,512]{3,2,1,0:T(8,128)S(1)}, u32[]{:S(2)}, u32[]{:S(2)}) collective-permute-start(f32[1,8,8,512]{3,2,1,0:T(8,128)S(1)} %get-tuple-element.37), channel_id=1, source_target_pairs={{0,16},{16,32},{32,48},{48,64},{64,80},{80,96},{96,112},{112,128},... | collective-permute-start | bytes 393224 | tf_op jit(solution)/shard_map/ppermute | solution.py:16
  298.9 6.3 %collective-permute-start.28 = (f32[1,8,8,512]{3,2,1,0:T(8,128)S(1)}, f32[1,8,8,512]{3,2,1,0:T(8,128)S(1)}, u32[]{:S(2)}, u32[]{:S(2)}) collective-permute-start(f32[1,8,8,512]{3,2,1,0:T(8,128)S(1)} %get-tuple-element.38), channel_id=1, source_target_pairs={{16,0},{32,16},{48,32},{64,48},{80,64},{96,80},{112,96},{128,112},... | collective-permute-start | bytes 393224 | tf_op jit(solution)/shard_map/ppermute | solution.py:19
  305.2 3.5 collective-permute-start.31
  306.6 6.1 %collective-permute-start.30 = (f32[10,1,8,512]{3,2,1,0:T(8,128)S(1)}, f32[10,1,8,512]{3,2,1,0:T(8,128)S(1)}, u32[]{:S(2)}, u32[]{:S(2)}) collective-permute-start(f32[10,1,8,512]{3,2,1,0:T(8,128)S(1)} %get-tuple-element.18), channel_id=1, source_target_pairs={{1,0},{2,1},{3,2},{4,3},{5,4},{6,5},{7,6},{8,7},{9,8},{10,9},{11,1... | collective-permute-start | bytes 491528 | tf_op jit(solution)/shard_map/ppermute | solution.py:19
  314.0 6.4 %collective-permute-start.33 = (f32[1,8,8,512]{3,2,1,0:T(8,128)S(1)}, f32[1,8,8,512]{3,2,1,0:T(8,128)S(1)}, u32[]{:S(2)}, u32[]{:S(2)}) collective-permute-start(f32[1,8,8,512]{3,2,1,0:T(8,128)S(1)} %get-tuple-element.35), channel_id=1, source_target_pairs={{0,16},{16,32},{32,48},{48,64},{64,80},{80,96},{96,112},{112,128},... | collective-permute-start | bytes 393224 | tf_op jit(solution)/shard_map/ppermute | solution.py:16
  318.5 6.3 %collective-permute-start.32 = (f32[1,8,8,512]{3,2,1,0:T(8,128)S(1)}, f32[1,8,8,512]{3,2,1,0:T(8,128)S(1)}, u32[]{:S(2)}, u32[]{:S(2)}) collective-permute-start(f32[1,8,8,512]{3,2,1,0:T(8,128)S(1)} %get-tuple-element.36), channel_id=1, source_target_pairs={{16,0},{32,16},{48,32},{64,48},{80,64},{96,80},{112,96},{128,112},... | collective-permute-start | bytes 393224 | tf_op jit(solution)/shard_map/ppermute | solution.py:19
  324.8 6.0 %collective-permute-start.35 = (f32[10,1,8,512]{3,2,1,0:T(8,128)S(1)}, f32[10,1,8,512]{3,2,1,0:T(8,128)S(1)}, u32[]{:S(2)}, u32[]{:S(2)}) collective-permute-start(f32[10,1,8,512]{3,2,1,0:T(8,128)S(1)} %get-tuple-element.15), channel_id=1, source_target_pairs={{0,1},{1,2},{2,3},{3,4},{4,5},{5,6},{6,7},{7,8},{8,9},{9,10},{10,1... | collective-permute-start | bytes 491528 | tf_op jit(solution)/shard_map/ppermute | solution.py:16
  328.6 6.1 %collective-permute-start.34 = (f32[10,1,8,512]{3,2,1,0:T(8,128)S(1)}, f32[10,1,8,512]{3,2,1,0:T(8,128)S(1)}, u32[]{:S(2)}, u32[]{:S(2)}) collective-permute-start(f32[10,1,8,512]{3,2,1,0:T(8,128)S(1)} %get-tuple-element.16), channel_id=1, source_target_pairs={{1,0},{2,1},{3,2},{4,3},{5,4},{6,5},{7,6},{8,7},{9,8},{10,9},{11,1... | collective-permute-start | bytes 491528 | tf_op jit(solution)/shard_map/ppermute | solution.py:19
  335.2 81.6 %copy-start.5 = (f32[8]{0:T(128)S(1)}, f32[8]{0:T(128)}, u32[]{:S(2)}) copy-start(f32[8]{0:T(128)} %copy-done.4) | copy-start | bytes 100
  418.3 4.3 collective-permute-start.37
  420.3 6.3 %collective-permute-start.36 = (f32[1,8,8,512]{3,2,1,0:T(8,128)S(1)}, f32[1,8,8,512]{3,2,1,0:T(8,128)S(1)}, u32[]{:S(2)}, u32[]{:S(2)}) collective-permute-start(f32[1,8,8,512]{3,2,1,0:T(8,128)S(1)} %get-tuple-element.34), channel_id=1, source_target_pairs={{16,0},{32,16},{48,32},{64,48},{80,64},{96,80},{112,96},{128,112},... | collective-permute-start | bytes 393224 | tf_op jit(solution)/shard_map/ppermute | solution.py:19
  426.7 3.8 collective-permute-start.39
  428.2 6.1 %collective-permute-start.38 = (f32[10,1,8,512]{3,2,1,0:T(8,128)S(1)}, f32[10,1,8,512]{3,2,1,0:T(8,128)S(1)}, u32[]{:S(2)}, u32[]{:S(2)}) collective-permute-start(f32[10,1,8,512]{3,2,1,0:T(8,128)S(1)} %get-tuple-element.14), channel_id=1, source_target_pairs={{1,0},{2,1},{3,2},{4,3},{5,4},{6,5},{7,6},{8,7},{9,8},{10,9},{11,1... | collective-permute-start | bytes 491528 | tf_op jit(solution)/shard_map/ppermute | solution.py:19
  434.9 81.5 %copy-start.3 = (f32[8]{0:T(128)S(1)}, f32[8]{0:T(128)}, u32[]{:S(2)}) copy-start(f32[8]{0:T(128)} %copy-done.2) | copy-start | bytes 100
where the time goes:
time: 521 us; the launch traced here: 519 us
  blocking collectives  286 us (55%)
  starting transfers between devices  110 us (21%)
  waiting for transfers between devices  90.7 us (17%)
  other arithmetic  25.9 us (5%)
    psum x2, blocking collectives, energy_sum(): return lax.psum(probe_dot(residual, precond), ('gx', 'gy'))  164 us
    ppermute x20, waiting for transfers between devices, with_halo(): lax.ppermute(lax.slice_in_dim(block, 0, width, axis=dim), axis, backward)  81.3 us
    psum x1, blocking collectives, body(): curvature = lax.psum(probe_dot(search, op_image), ('gx', 'gy'))  79.8 us
    ppermute x20, starting transfers between devices, with_halo(): lax.ppermute(lax.slice_in_dim(block, block.shape[dim] - width, None, axis...  77 us
    all_gather x2, blocking collectives, coarse_solve(): lax.all_gather(local_means, 'gy', axis=1, tiled=True)  42.5 us
    ppermute x20, starting transfers between devices, with_halo(): lax.ppermute(lax.slice_in_dim(block, 0, width, axis=dim), axis, backward)  33 us
  transfers between devices with their start and end apart: 40, of which 30 were waited for; matrix products, arithmetic and copies ran while one was open for 0% of the time, Pallas kernels for 0%

commit v1 on v0

--- a/solution.py
+++ b/solution.py
@@ -85,7 +85,7 @@
 
 
 def energy_sum(residual, precond):
-    return lax.psum(probe_dot(residual, precond), ("gx", "gy"))
+    return lax.psum(lax.psum(probe_dot(residual, precond), "gy"), "gx")
 
 
 def body(right_side, kappa_sq, coarse_inverse):

time: 521 us -> 561 us (1.077)
  blocking collectives: 286 us -> 325 us
    psum x1 -> x2, blocking collectives: 79.8 us -> 169 us  [body(): curvature = lax.psum(probe_dot(search, op_image), ('gx', 'gy'))]
    psum x2 -> x4, blocking collectives: 164 us -> 114 us  [energy_sum(): return lax.psum(lax.psum(probe_dot(residual, precond), 'gy'), 'gx')]
where the time goes in v1:
time: 561 us; the launch traced here: 559 us
  blocking collectives  325 us (58%)
  starting transfers between devices  110 us (20%)
  waiting for transfers between devices  90.7 us (16%)
  other arithmetic  25.9 us (5%)
    psum x2, blocking collectives, body(): curvature = lax.psum(probe_dot(search, op_image), ('gx', 'gy'))  169 us
    psum x4, blocking collectives, energy_sum(): return lax.psum(lax.psum(probe_dot(residual, precond), 'gy'), 'gx')  114 us
    ppermute x20, waiting for transfers between devices, with_halo(): lax.ppermute(lax.slice_in_dim(block, 0, width, axis=dim), axis, backward)  81.1 us
    ppermute x20, starting transfers between devices, with_halo(): lax.ppermute(lax.slice_in_dim(block, block.shape[dim] - width, None, axis...  76.8 us
    all_gather x2, blocking collectives, coarse_solve(): lax.all_gather(local_means, 'gy', axis=1, tiled=True)  42.4 us
    ppermute x20, starting transfers between devices, with_halo(): lax.ppermute(lax.slice_in_dim(block, 0, width, axis=dim), axis, backward)  33.5 us
  transfers between devices with their start and end apart: 40, of which 30 were waited for; matrix products, arithmetic and copies ran while one was open for 0% of the time, Pallas kernels for 0%

profile of v1, /device:TPU:1, one launch (start us, length us, event | category | flops | bytes accessed | tf_op | source)
XLA Modules:
  0.0 558.9 jit_solution(9475435423449159611)
XLA Ops:
  3.1 4.9 collective-permute-start.1
  8.0 1.9 collective-permute-start
  9.9 4.3 collective-permute-done
  14.3 3.3 collective-permute-start.3
  19.8 3.8 collective-permute-done.2
  25.0 4.1 collective-permute-start.5
  29.1 1.9 collective-permute-start.4
  31.0 4.3 collective-permute-done.4
  35.4 3.1 collective-permute-start.7
  40.7 3.8 collective-permute-done.6
  46.0 21.1 %all-gather = f32[16,16,8]{1,2,0:T(8,128)S(1)} all-gather(f32[1,16,8]{1,2,0:T(8,128)S(1)} %multiply_bitcast_fusion.1), channel_id=1, replica_groups=mesh['gx'=16,'gy'=16] {'gy'}, dimensions={0}, use_global_device_ids=true | all-gather | bytes 8704 | tf_op jit(solution)/shard_map/all_gather | solution.py:51
  67.6 9.0 %collective-permute-start.9 = (f32[1,8,8,512]{3,2,1,0:T(8,128)S(1)}, f32[1,8,8,512]{3,2,1,0:T(8,128)S(1)}, u32[]{:S(2)}, u32[]{:S(2)}) collective-permute-start(f32[1,8,8,512]{3,2,1,0:T(8,128)S(1)} %get-tuple-element.45), channel_id=1, source_target_pairs={{0,16},{16,32},{32,48},{48,64},{64,80},{80,96},{96,112},{112,128},... | collective-permute-start | bytes 393224 | tf_op jit(solution)/shard_map/ppermute | solution.py:16
  76.6 1.9 collective-permute-start.8
  78.5 4.3 collective-permute-done.8
  82.9 1.8 collective-permute-start.11
  87.0 3.8 collective-permute-done.10
  92.1 4.7 collective-permute-start.13
  96.8 1.9 collective-permute-start.12
  98.7 4.3 collective-permute-done.12
  103.1 2.8 collective-permute-start.15
  108.2 3.8 collective-permute-done.14
  113.3 4.0 collective-permute-start.17
  117.3 1.9 collective-permute-start.16
  119.3 4.3 collective-permute-done.16
  123.7 4.9 collective-permute-start.19
  130.8 3.8 collective-permute-done.18
  135.2 1.8 multiply_reduce_fusion.2
  137.0 30.6 %psum.42 = f32[8]{0:T(128)S(1)} all-reduce(f32[8]{0:T(128)S(1)} %get-tuple-element.3), channel_id=1, replica_groups=mesh['gx'=16,'gy'=16] {'gy'}, use_global_device_ids=true, to_apply=%region_3.4 | all-reduce | flops 8 | bytes 64 | tf_op jit(solution)/shard_map/psum | solution.py:88
  167.6 83.5 %psum.44 = f32[8]{0:T(128)S(1)} all-reduce(f32[8]{0:T(128)S(1)} %get-tuple-element.2), channel_id=1, replica_groups=mesh['gx'=16,'gy'=16] {'gx','gy'}, use_global_device_ids=true, to_apply=%region_6.7 | all-reduce | flops 8 | bytes 64 | tf_op jit(solution)/shard_map/psum | solution.py:100
  251.1 24.0 %psum.43 = f32[8]{0:T(128)S(1)} all-reduce(f32[8]{0:T(128)S(1)} %psum.42), channel_id=1, replica_groups=mesh['gx'=16,'gy'=16] {'gx'}, use_global_device_ids=true, to_apply=%region_4.5 | all-reduce | flops 8 | bytes 64 | tf_op jit(solution)/shard_map/psum | solution.py:88
  275.6 1.6 multiply_divide_fusion
  277.2 3.0 collective-permute-start.21
  280.2 3.1 collective-permute-start.20
  283.4 3.1 collective-permute-done.20
  286.5 3.2 collective-permute-start.23
  289.7 1.5 collective-permute-start.22
  292.3 4.1 collective-permute-done.22
  297.7 2.5 collective-permute-start.25
  300.3 1.9 collective-permute-start.24
  302.2 4.3 collective-permute-done.24
  306.6 2.2 collective-permute-start.27
  311.1 4.1 collective-permute-done.26
  318.1 21.4 %all-gather.1 = f32[16,16,8]{1,2,0:T(8,128)S(1)} all-gather(f32[1,16,8]{1,2,0:T(8,128)S(1)} %multiply_bitcast_fusion), channel_id=1, replica_groups=mesh['gx'=16,'gy'=16] {'gy'}, dimensions={0}, use_global_device_ids=true | all-gather | bytes 8704 | tf_op jit(solution)/shard_map/all_gather | solution.py:51
  342.9 8.6 %collective-permute-start.29 = (f32[1,8,8,512]{3,2,1,0:T(8,128)S(1)}, f32[1,8,8,512]{3,2,1,0:T(8,128)S(1)}, u32[]{:S(2)}, u32[]{:S(2)}) collective-permute-start(f32[1,8,8,512]{3,2,1,0:T(8,128)S(1)} %get-tuple-element.35), channel_id=1, source_target_pairs={{0,16},{16,32},{32,48},{48,64},{64,80},{80,96},{96,112},{112,128},... | collective-permute-start | bytes 393224 | tf_op jit(solution)/shard_map/ppermute | solution.py:16
  351.5 1.9 collective-permute-start.28
  353.4 4.3 collective-permute-done.28
  361.3 3.8 collective-permute-done.30
  366.5 3.9 collective-permute-start.33
  370.4 1.9 collective-permute-start.32
  372.4 4.3 collective-permute-done.32
  376.8 3.4 collective-permute-start.35
  382.4 3.8 collective-permute-done.34
  386.8 1.8 multiply_reduce_fusion.1
  388.6 30.1 %psum.45 = f32[8]{0:T(128)S(1)} all-reduce(f32[8]{0:T(128)S(1)} %get-tuple-element.6), channel_id=1, replica_groups=mesh['gx'=16,'gy'=16] {'gy'}, use_global_device_ids=true, to_apply=%region_10.11 | all-reduce | flops 8 | bytes 64 | tf_op jit(solution)/shard_map/psum | solution.py:88
  418.7 29.3 %psum.46 = f32[8]{0:T(128)S(1)} all-reduce(f32[8]{0:T(128)S(1)} %psum.45), channel_id=1, replica_groups=mesh['gx'=16,'gy'=16] {'gx'}, use_global_device_ids=true, to_apply=%region_11.12 | all-reduce | flops 8 | bytes 64 | tf_op jit(solution)/shard_map/psum | solution.py:88
  448.0 1.5 multiply_add_fusion.1
  449.6 4.1 collective-permute-start.37
  453.7 1.9 collective-permute-start.36
  455.7 4.3 collective-permute-done.36
  460.1 2.1 collective-permute-start.39
  464.4 3.8 collective-permute-done.38
  468.8 1.7 multiply_reduce_fusion
  470.5 85.4 %psum.47 = f32[8]{0:T(128)S(1)} all-reduce(f32[8]{0:T(128)S(1)} %get-tuple-element.4), channel_id=1, replica_groups=mesh['gx'=16,'gy'=16] {'gx','gy'}, use_global_device_ids=true, to_apply=%region_13.14 | all-reduce | flops 8 | bytes 64 | tf_op jit(solution)/shard_map/psum | solution.py:100
  555.8 3.1 multiply_subtract_fusion
  (102 shorter events, 42.3 us)
Async XLA Ops:
  0.6 66.5 %copy-start = (f32[256,256]{1,0:T(8,128)S(1)}, f32[256,256]{1,0:T(8,128)}, u32[]{:S(2)}) copy-start(f32[256,256]{1,0:T(8,128)} %param.5) | copy-start | bytes 786436
  3.1 6.9 %collective-permute-start.1 = (f32[1,8,8,512]{3,2,1,0:T(8,128)S(1)}, f32[1,8,8,512]{3,2,1,0:T(8,128)S(1)}, u32[]{:S(2)}, u32[]{:S(2)}) collective-permute-start(f32[1,8,8,512]{3,2,1,0:T(8,128)S(1)} %get-tuple-element.49), channel_id=1, source_target_pairs={{0,16},{16,32},{32,48},{48,64},{64,80},{80,96},{96,112},{112,128},... | collective-permute-start | bytes 393224 | tf_op jit(solution)/shard_map/ppermute | solution.py:16
  8.0 6.3 %collective-permute-start = (f32[1,8,8,512]{3,2,1,0:T(8,128)S(1)}, f32[1,8,8,512]{3,2,1,0:T(8,128)S(1)}, u32[]{:S(2)}, u32[]{:S(2)}) collective-permute-start(f32[1,8,8,512]{3,2,1,0:T(8,128)S(1)} %get-tuple-element.50), channel_id=1, source_target_pairs={{16,0},{32,16},{48,32},{64,48},{80,64},{96,80},{112,96},{128,112},... | collective-permute-start | bytes 393224 | tf_op jit(solution)/shard_map/ppermute | solution.py:19
  14.3 9.9 %copy-start.1 = (f32[8,8,8,512]{3,2,1,0:T(8,128)S(1)}, f32[8,8,8,512]{3,2,1,0:T(8,128)}, u32[]{:S(2)}) copy-start(f32[8,8,8,512]{3,2,1,0:T(8,128)} %param.3) | copy-start | bytes 3145732
  14.3 5.5 collective-permute-start.3
  17.6 6.1 %collective-permute-start.2 = (f32[10,1,8,512]{3,2,1,0:T(8,128)S(1)}, f32[10,1,8,512]{3,2,1,0:T(8,128)S(1)}, u32[]{:S(2)}, u32[]{:S(2)}) collective-permute-start(f32[10,1,8,512]{3,2,1,0:T(8,128)S(1)} %get-tuple-element.30), channel_id=1, source_target_pairs={{1,0},{2,1},{3,2},{4,3},{5,4},{6,5},{7,6},{8,7},{9,8},{10,9},{11,1... | collective-permute-start | bytes 491528 | tf_op jit(solution)/shard_map/ppermute | solution.py:19
  25.0 6.0 %collective-permute-start.5 = (f32[1,8,8,512]{3,2,1,0:T(8,128)S(1)}, f32[1,8,8,512]{3,2,1,0:T(8,128)S(1)}, u32[]{:S(2)}, u32[]{:S(2)}) collective-permute-start(f32[1,8,8,512]{3,2,1,0:T(8,128)S(1)} %get-tuple-element.47), channel_id=1, source_target_pairs={{0,16},{16,32},{32,48},{48,64},{64,80},{80,96},{96,112},{112,128},... | collective-permute-start | bytes 393224 | tf_op jit(solution)/shard_map/ppermute | solution.py:16
  29.1 6.3 %collective-permute-start.4 = (f32[1,8,8,512]{3,2,1,0:T(8,128)S(1)}, f32[1,8,8,512]{3,2,1,0:T(8,128)S(1)}, u32[]{:S(2)}, u32[]{:S(2)}) collective-permute-start(f32[1,8,8,512]{3,2,1,0:T(8,128)S(1)} %get-tuple-element.48), channel_id=1, source_target_pairs={{16,0},{32,16},{48,32},{64,48},{80,64},{96,80},{112,96},{128,112},... | collective-permute-start | bytes 393224 | tf_op jit(solution)/shard_map/ppermute | solution.py:19
  35.4 5.4 collective-permute-start.7
  38.5 6.1 %collective-permute-start.6 = (f32[10,1,8,512]{3,2,1,0:T(8,128)S(1)}, f32[10,1,8,512]{3,2,1,0:T(8,128)S(1)}, u32[]{:S(2)}, u32[]{:S(2)}) collective-permute-start(f32[10,1,8,512]{3,2,1,0:T(8,128)S(1)} %get-tuple-element.28), channel_id=1, source_target_pairs={{1,0},{2,1},{3,2},{4,3},{5,4},{6,5},{7,6},{8,7},{9,8},{10,9},{11,1... | collective-permute-start | bytes 491528 | tf_op jit(solution)/shard_map/ppermute | solution.py:19
  67.6 10.9 %collective-permute-start.9 = (f32[1,8,8,512]{3,2,1,0:T(8,128)S(1)}, f32[1,8,8,512]{3,2,1,0:T(8,128)S(1)}, u32[]{:S(2)}, u32[]{:S(2)}) collective-permute-start(f32[1,8,8,512]{3,2,1,0:T(8,128)S(1)} %get-tuple-element.45), channel_id=1, source_target_pairs={{0,16},{16,32},{32,48},{48,64},{64,80},{80,96},{96,112},{112,128},... | collective-permute-start | bytes 393224 | tf_op jit(solution)/shard_map/ppermute | solution.py:16
  76.6 6.3 %collective-permute-start.8 = (f32[1,8,8,512]{3,2,1,0:T(8,128)S(1)}, f32[1,8,8,512]{3,2,1,0:T(8,128)S(1)}, u32[]{:S(2)}, u32[]{:S(2)}) collective-permute-start(f32[1,8,8,512]{3,2,1,0:T(8,128)S(1)} %get-tuple-element.46), channel_id=1, source_target_pairs={{16,0},{32,16},{48,32},{64,48},{80,64},{96,80},{112,96},{128,112},... | collective-permute-start | bytes 393224 | tf_op jit(solution)/shard_map/ppermute | solution.py:19
  82.9 4.1 collective-permute-start.11
  84.7 6.1 %collective-permute-start.10 = (f32[10,1,8,512]{3,2,1,0:T(8,128)S(1)}, f32[10,1,8,512]{3,2,1,0:T(8,128)S(1)}, u32[]{:S(2)}, u32[]{:S(2)}) collective-permute-start(f32[10,1,8,512]{3,2,1,0:T(8,128)S(1)} %get-tuple-element.26), channel_id=1, source_target_pairs={{1,0},{2,1},{3,2},{4,3},{5,4},{6,5},{7,6},{8,7},{9,8},{10,9},{11,1... | collective-permute-start | bytes 491528 | tf_op jit(solution)/shard_map/ppermute | solution.py:19
  92.1 6.6 %collective-permute-start.13 = (f32[1,8,8,512]{3,2,1,0:T(8,128)S(1)}, f32[1,8,8,512]{3,2,1,0:T(8,128)S(1)}, u32[]{:S(2)}, u32[]{:S(2)}) collective-permute-start(f32[1,8,8,512]{3,2,1,0:T(8,128)S(1)} %get-tuple-element.43), channel_id=1, source_target_pairs={{0,16},{16,32},{32,48},{48,64},{64,80},{80,96},{96,112},{112,128},... | collective-permute-start | bytes 393224 | tf_op jit(solution)/shard_map/ppermute | solution.py:16
  96.8 6.3 %collective-permute-start.12 = (f32[1,8,8,512]{3,2,1,0:T(8,128)S(1)}, f32[1,8,8,512]{3,2,1,0:T(8,128)S(1)}, u32[]{:S(2)}, u32[]{:S(2)}) collective-permute-start(f32[1,8,8,512]{3,2,1,0:T(8,128)S(1)} %get-tuple-element.44), channel_id=1, source_target_pairs={{16,0},{32,16},{48,32},{64,48},{80,64},{96,80},{112,96},{128,112},... | collective-permute-start | bytes 393224 | tf_op jit(solution)/shard_map/ppermute | solution.py:19
  103.1 5.1 collective-permute-start.15
  106.0 6.1 %collective-permute-start.14 = (f32[10,1,8,512]{3,2,1,0:T(8,128)S(1)}, f32[10,1,8,512]{3,2,1,0:T(8,128)S(1)}, u32[]{:S(2)}, u32[]{:S(2)}) collective-permute-start(f32[10,1,8,512]{3,2,1,0:T(8,128)S(1)} %get-tuple-element.24), channel_id=1, source_target_pairs={{1,0},{2,1},{3,2},{4,3},{5,4},{6,5},{7,6},{8,7},{9,8},{10,9},{11,1... | collective-permute-start | bytes 491528 | tf_op jit(solution)/shard_map/ppermute | solution.py:19
  113.3 5.9 %collective-permute-start.17 = (f32[1,8,8,512]{3,2,1,0:T(8,128)S(1)}, f32[1,8,8,512]{3,2,1,0:T(8,128)S(1)}, u32[]{:S(2)}, u32[]{:S(2)}) collective-permute-start(f32[1,8,8,512]{3,2,1,0:T(8,128)S(1)} %get-tuple-element.41), channel_id=1, source_target_pairs={{0,16},{16,32},{32,48},{48,64},{64,80},{80,96},{96,112},{112,128},... | collective-permute-start | bytes 393224 | tf_op jit(solution)/shard_map/ppermute | solution.py:16
  117.3 6.3 %collective-permute-start.16 = (f32[1,8,8,512]{3,2,1,0:T(8,128)S(1)}, f32[1,8,8,512]{3,2,1,0:T(8,128)S(1)}, u32[]{:S(2)}, u32[]{:S(2)}) collective-permute-start(f32[1,8,8,512]{3,2,1,0:T(8,128)S(1)} %get-tuple-element.42), channel_id=1, source_target_pairs={{16,0},{32,16},{48,32},{64,48},{80,64},{96,80},{112,96},{128,112},... | collective-permute-start | bytes 393224 | tf_op jit(solution)/shard_map/ppermute | solution.py:19
  123.7 7.1 %collective-permute-start.19 = (f32[10,1,8,512]{3,2,1,0:T(8,128)S(1)}, f32[10,1,8,512]{3,2,1,0:T(8,128)S(1)}, u32[]{:S(2)}, u32[]{:S(2)}) collective-permute-start(f32[10,1,8,512]{3,2,1,0:T(8,128)S(1)} %get-tuple-element.21), channel_id=1, source_target_pairs={{0,1},{1,2},{2,3},{3,4},{4,5},{5,6},{6,7},{7,8},{8,9},{9,10},{10,1... | collective-permute-start | bytes 491528 | tf_op jit(solution)/shard_map/ppermute | solution.py:16
  128.5 6.1 %collective-permute-start.18 = (f32[10,1,8,512]{3,2,1,0:T(8,128)S(1)}, f32[10,1,8,512]{3,2,1,0:T(8,128)S(1)}, u32[]{:S(2)}, u32[]{:S(2)}) collective-permute-start(f32[10,1,8,512]{3,2,1,0:T(8,128)S(1)} %get-tuple-element.22), channel_id=1, source_target_pairs={{1,0},{2,1},{3,2},{4,3},{5,4},{6,5},{7,6},{8,7},{9,8},{10,9},{11,1... | collective-permute-start | bytes 491528 | tf_op jit(solution)/shard_map/ppermute | solution.py:19
  275.1 0.5 copy-start.4
  275.6 1.6 copy-start.2
  277.2 6.1 %collective-permute-start.21 = (f32[1,8,8,512]{3,2,1,0:T(8,128)S(1)}, f32[1,8,8,512]{3,2,1,0:T(8,128)S(1)}, u32[]{:S(2)}, u32[]{:S(2)}) collective-permute-start(f32[1,8,8,512]{3,2,1,0:T(8,128)S(1)} %get-tuple-element.39), channel_id=1, source_target_pairs={{0,16},{16,32},{32,48},{48,64},{64,80},{80,96},{96,112},{112,128},... | collective-permute-start | bytes 393224 | tf_op jit(solution)/shard_map/ppermute | solution.py:16
  280.2 6.3 %collective-permute-start.20 = (f32[1,8,8,512]{3,2,1,0:T(8,128)S(1)}, f32[1,8,8,512]{3,2,1,0:T(8,128)S(1)}, u32[]{:S(2)}, u32[]{:S(2)}) collective-permute-start(f32[1,8,8,512]{3,2,1,0:T(8,128)S(1)} %get-tuple-element.40), channel_id=1, source_target_pairs={{16,0},{32,16},{48,32},{64,48},{80,64},{96,80},{112,96},{128,112},... | collective-permute-start | bytes 393224 | tf_op jit(solution)/shard_map/ppermute | solution.py:19
  286.5 5.8 %collective-permute-start.23 = (f32[10,1,8,512]{3,2,1,0:T(8,128)S(1)}, f32[10,1,8,512]{3,2,1,0:T(8,128)S(1)}, u32[]{:S(2)}, u32[]{:S(2)}) collective-permute-start(f32[10,1,8,512]{3,2,1,0:T(8,128)S(1)} %get-tuple-element.19), channel_id=1, source_target_pairs={{0,1},{1,2},{2,3},{3,4},{4,5},{5,6},{6,7},{7,8},{8,9},{9,10},{10,1... | collective-permute-start | bytes 491528 | tf_op jit(solution)/shard_map/ppermute | solution.py:16
  289.7 6.7 %collective-permute-start.22 = (f32[10,1,8,512]{3,2,1,0:T(8,128)S(1)}, f32[10,1,8,512]{3,2,1,0:T(8,128)S(1)}, u32[]{:S(2)}, u32[]{:S(2)}) collective-permute-start(f32[10,1,8,512]{3,2,1,0:T(8,128)S(1)} %get-tuple-element.20), channel_id=1, source_target_pairs={{1,0},{2,1},{3,2},{4,3},{5,4},{6,5},{7,6},{8,7},{9,8},{10,9},{11,1... | collective-permute-start | bytes 491528 | tf_op jit(solution)/shard_map/ppermute | solution.py:19
  297.7 4.5 collective-permute-start.25
  300.3 6.3 %collective-permute-start.24 = (f32[1,8,8,512]{3,2,1,0:T(8,128)S(1)}, f32[1,8,8,512]{3,2,1,0:T(8,128)S(1)}, u32[]{:S(2)}, u32[]{:S(2)}) collective-permute-start(f32[1,8,8,512]{3,2,1,0:T(8,128)S(1)} %get-tuple-element.38), channel_id=1, source_target_pairs={{16,0},{32,16},{48,32},{64,48},{80,64},{96,80},{112,96},{128,112},... | collective-permute-start | bytes 393224 | tf_op jit(solution)/shard_map/ppermute | solution.py:19
  306.6 4.5 collective-permute-start.27
  308.8 6.3 %collective-permute-start.26 = (f32[10,1,8,512]{3,2,1,0:T(8,128)S(1)}, f32[10,1,8,512]{3,2,1,0:T(8,128)S(1)}, u32[]{:S(2)}, u32[]{:S(2)}) collective-permute-start(f32[10,1,8,512]{3,2,1,0:T(8,128)S(1)} %get-tuple-element.18), channel_id=1, source_target_pairs={{1,0},{2,1},{3,2},{4,3},{5,4},{6,5},{7,6},{8,7},{9,8},{10,9},{11,1... | collective-permute-start | bytes 491528 | tf_op jit(solution)/shard_map/ppermute | solution.py:19
  342.9 10.5 %collective-permute-start.29 = (f32[1,8,8,512]{3,2,1,0:T(8,128)S(1)}, f32[1,8,8,512]{3,2,1,0:T(8,128)S(1)}, u32[]{:S(2)}, u32[]{:S(2)}) collective-permute-start(f32[1,8,8,512]{3,2,1,0:T(8,128)S(1)} %get-tuple-element.35), channel_id=1, source_target_pairs={{0,16},{16,32},{32,48},{48,64},{64,80},{80,96},{96,112},{112,128},... | collective-permute-start | bytes 393224 | tf_op jit(solution)/shard_map/ppermute | solution.py:16
  351.5 6.3 %collective-permute-start.28 = (f32[1,8,8,512]{3,2,1,0:T(8,128)S(1)}, f32[1,8,8,512]{3,2,1,0:T(8,128)S(1)}, u32[]{:S(2)}, u32[]{:S(2)}) collective-permute-start(f32[1,8,8,512]{3,2,1,0:T(8,128)S(1)} %get-tuple-element.36), channel_id=1, source_target_pairs={{16,0},{32,16},{48,32},{64,48},{80,64},{96,80},{112,96},{128,112},... | collective-permute-start | bytes 393224 | tf_op jit(solution)/shard_map/ppermute | solution.py:19
  357.8 3.5 collective-permute-start.31
  359.1 6.1 %collective-permute-start.30 = (f32[10,1,8,512]{3,2,1,0:T(8,128)S(1)}, f32[10,1,8,512]{3,2,1,0:T(8,128)S(1)}, u32[]{:S(2)}, u32[]{:S(2)}) collective-permute-start(f32[10,1,8,512]{3,2,1,0:T(8,128)S(1)} %get-tuple-element.16), channel_id=1, source_target_pairs={{1,0},{2,1},{3,2},{4,3},{5,4},{6,5},{7,6},{8,7},{9,8},{10,9},{11,1... | collective-permute-start | bytes 491528 | tf_op jit(solution)/shard_map/ppermute | solution.py:19
  366.5 5.9 %collective-permute-start.33 = (f32[1,8,8,512]{3,2,1,0:T(8,128)S(1)}, f32[1,8,8,512]{3,2,1,0:T(8,128)S(1)}, u32[]{:S(2)}, u32[]{:S(2)}) collective-permute-start(f32[1,8,8,512]{3,2,1,0:T(8,128)S(1)} %get-tuple-element.33), channel_id=1, source_target_pairs={{0,16},{16,32},{32,48},{48,64},{64,80},{80,96},{96,112},{112,128},... | collective-permute-start | bytes 393224 | tf_op jit(solution)/shard_map/ppermute | solution.py:16
  370.4 6.3 %collective-permute-start.32 = (f32[1,8,8,512]{3,2,1,0:T(8,128)S(1)}, f32[1,8,8,512]{3,2,1,0:T(8,128)S(1)}, u32[]{:S(2)}, u32[]{:S(2)}) collective-permute-start(f32[1,8,8,512]{3,2,1,0:T(8,128)S(1)} %get-tuple-element.34), channel_id=1, source_target_pairs={{16,0},{32,16},{48,32},{64,48},{80,64},{96,80},{112,96},{128,112},... | collective-permute-start | bytes 393224 | tf_op jit(solution)/shard_map/ppermute | solution.py:19
  376.8 5.6 %collective-permute-start.35 = (f32[10,1,8,512]{3,2,1,0:T(8,128)S(1)}, f32[10,1,8,512]{3,2,1,0:T(8,128)S(1)}, u32[]{:S(2)}, u32[]{:S(2)}) collective-permute-start(f32[10,1,8,512]{3,2,1,0:T(8,128)S(1)} %get-tuple-element.13), channel_id=1, source_target_pairs={{0,1},{1,2},{2,3},{3,4},{4,5},{5,6},{6,7},{7,8},{8,9},{9,10},{10,1... | collective-permute-start | bytes 491528 | tf_op jit(solution)/shard_map/ppermute | solution.py:16
  380.1 6.1 %collective-permute-start.34 = (f32[10,1,8,512]{3,2,1,0:T(8,128)S(1)}, f32[10,1,8,512]{3,2,1,0:T(8,128)S(1)}, u32[]{:S(2)}, u32[]{:S(2)}) collective-permute-start(f32[10,1,8,512]{3,2,1,0:T(8,128)S(1)} %get-tuple-element.14), channel_id=1, source_target_pairs={{1,0},{2,1},{3,2},{4,3},{5,4},{6,5},{7,6},{8,7},{9,8},{10,9},{11,1... | collective-permute-start | bytes 491528 | tf_op jit(solution)/shard_map/ppermute | solution.py:19
  386.8 61.2 %copy-start.5 = (f32[8]{0:T(128)S(1)}, f32[8]{0:T(128)}, u32[]{:S(2)}) copy-start(f32[8]{0:T(128)} %copy-done.4) | copy-start | bytes 100
  449.6 6.1 %collective-permute-start.37 = (f32[1,8,8,512]{3,2,1,0:T(8,128)S(1)}, f32[1,8,8,512]{3,2,1,0:T(8,128)S(1)}, u32[]{:S(2)}, u32[]{:S(2)}) collective-permute-start(f32[1,8,8,512]{3,2,1,0:T(8,128)S(1)} %get-tuple-element.31), channel_id=1, source_target_pairs={{0,16},{16,32},{32,48},{48,64},{64,80},{80,96},{96,112},{112,128},... | collective-permute-start | bytes 393224 | tf_op jit(solution)/shard_map/ppermute | solution.py:16
  453.7 6.3 %collective-permute-start.36 = (f32[1,8,8,512]{3,2,1,0:T(8,128)S(1)}, f32[1,8,8,512]{3,2,1,0:T(8,128)S(1)}, u32[]{:S(2)}, u32[]{:S(2)}) collective-permute-start(f32[1,8,8,512]{3,2,1,0:T(8,128)S(1)} %get-tuple-element.32), channel_id=1, source_target_pairs={{16,0},{32,16},{48,32},{64,48},{80,64},{96,80},{112,96},{128,112},... | collective-permute-start | bytes 393224 | tf_op jit(solution)/shard_map/ppermute | solution.py:19
  460.1 4.3 collective-permute-start.39
  462.1 6.1 %collective-permute-start.38 = (f32[10,1,8,512]{3,2,1,0:T(8,128)S(1)}, f32[10,1,8,512]{3,2,1,0:T(8,128)S(1)}, u32[]{:S(2)}, u32[]{:S(2)}) collective-permute-start(f32[10,1,8,512]{3,2,1,0:T(8,128)S(1)} %get-tuple-element.12), channel_id=1, source_target_pairs={{1,0},{2,1},{3,2},{4,3},{5,4},{6,5},{7,6},{8,7},{9,8},{10,9},{11,1... | collective-permute-start | bytes 491528 | tf_op jit(solution)/shard_map/ppermute | solution.py:19
  468.8 87.0 %copy-start.3 = (f32[8]{0:T(128)S(1)}, f32[8]{0:T(128)}, u32[]{:S(2)}) copy-start(f32[8]{0:T(128)} %copy-done.2) | copy-start | bytes 100
